TPU v7x, 32 devices: a whole 2x2x4 slice. The times are simulated.
32 devices in a mesh: island: 4 (over y, core), fsdp: 8 (over z, x).
Axes of the slice: x: 2, y: 2, z: 4, core: 2. Of those that a mesh axis runs over, the one named last changes fastest.
Arguments:
- params: float32 [4, 128, 2, 6656], P('island', 'fsdp'), may hold values from -40 to 40
- adam_m: float32 [4, 128, 2, 6656], P('island', 'fsdp'), may hold values from -3 to 3
- adam_v: float32 [4, 128, 2, 6656], P('island', 'fsdp'), may hold values from 0.1 to 4
- outer_params: float32 [128, 2, 6656], P('fsdp'), may hold values from -6 to 6
- outer_mom: float32 [128, 2, 6656], P('fsdp'), may hold values from -3 to 3
- obs_ids: int32 [4, 4096], P('island', 'fsdp'), may hold values from 0 to 127
- act_ids: int32 [4, 4096], P('island', 'fsdp'), may hold values from 0 to 127
- fragment: int32 [1], replicated, may hold values from 0 to 51
Outputs:
- new_params: float32 [4, 128, 2, 6656], P('island', 'fsdp')
- new_moment: float32 [4, 128, 2, 6656], P('island', 'fsdp')
- new_second: float32 [4, 128, 2, 6656], P('island', 'fsdp')
- new_outer: float32 [128, 2, 6656], P('fsdp')
- new_outer_mom: float32 [128, 2, 6656], P('fsdp')
All inputs are finite; a program needn't handle non-finite values.
Results may differ from a plain program's by a relative error of at most 0.0095.
Values may be sent and summed in bfloat16 or wider, within the bound.
A program may use at most 64 MiB of HBM per device.

v0:
```python
import math

import jax
import jax.numpy as jnp
from jax import lax
from jax.sharding import PartitionSpec as P

FRAG_COLS = 128


beta_first = 0.8
beta_second = 0.95
inner_rate = 0.05
decay_rate = 0.1
adam_eps = 1e-08
outer_rate = 0.7
outer_beta = 0.9
mix_weight = 0.5
norm_eps = 1e-06


def on_device(params, adam_m, adam_v, outer_params, outer_mom, obs_ids, act_ids, fragment):
    tables = params[0]
    tables_b = tables.astype(jnp.bfloat16)
    model_width = tables.shape[-1]
    shard_rows = tables.shape[0]
    vocab_rows = shard_rows * lax.axis_size("fsdp")
    islands = lax.axis_size("island")
    logit_scale = 2.0 / math.sqrt(model_width)
    offset = fragment[0] * FRAG_COLS
    outer_slice = lax.dynamic_slice_in_dim(outer_params, offset, FRAG_COLS, 2)
    mom_slice = lax.dynamic_slice_in_dim(outer_mom, offset, FRAG_COLS, 2)
    drifts = outer_slice - lax.dynamic_slice_in_dim(tables, offset, FRAG_COLS, 2)
    mean_drift = lax.psum(drifts, "island") / islands
    new_mom_slice = outer_beta * mom_slice + mean_drift
    new_outer_slice = outer_slice - outer_rate * (mean_drift + outer_beta * new_mom_slice)
    obs_rows = obs_ids[0]
    act_rows = act_ids[0]
    columns = lax.broadcasted_iota(jnp.int32, (obs_rows.shape[0], vocab_rows), 1)
    obs_hot = (obs_rows[:, None] == columns).astype(jnp.bfloat16)
    target_hot = (act_rows[:, None] == columns).astype(jnp.float32)
    gathered = lax.all_gather(tables_b, "fsdp", axis=0, tiled=True)
    embedded = jnp.dot(obs_hot, gathered[:, 0, :], preferred_element_type=jnp.float32)
    head_rows = gathered[:, 1, :]
    inv_rms = lax.rsqrt(jnp.mean(embedded * embedded, axis=-1, keepdims=True) + norm_eps)
    unit_rows = embedded * inv_rms
    normed = unit_rows.astype(jnp.bfloat16)
    logits = (
        jnp.einsum("td,ad->ta", normed, head_rows, preferred_element_type=jnp.float32) * logit_scale
    )
    largest = jnp.max(logits, axis=-1, keepdims=True)
    expon = jnp.exp(logits - largest)
    probs = expon / jnp.sum(expon, axis=-1, keepdims=True)
    dlogits = (probs - target_hot).astype(jnp.bfloat16)
    dnormed = jnp.dot(dlogits, head_rows, preferred_element_type=jnp.float32) * logit_scale
    dembedded = (
        inv_rms * (dnormed - unit_rows * jnp.mean(dnormed * unit_rows, axis=-1, keepdims=True))
    ).astype(jnp.bfloat16)
    head_term = (
        jnp.einsum("ta,td->ad", dlogits, normed, preferred_element_type=jnp.float32) * logit_scale
    )
    embed_term = jnp.einsum("ta,td->ad", obs_hot, dembedded, preferred_element_type=jnp.float32)
    gradient = lax.psum_scatter(
        jnp.stack([embed_term, head_term], axis=1).astype(jnp.bfloat16),
        "fsdp",
        scatter_dimension=0,
        tiled=True,
    ).astype(jnp.float32)
    new_moment = beta_first * adam_m[0] + (1.0 - beta_first) * gradient
    new_second = beta_second * adam_v[0] + (1.0 - beta_second) * gradient * gradient
    stepped = tables - inner_rate * (
        new_moment / (jnp.sqrt(new_second) + adam_eps) + decay_rate * tables
    )
    stepped_slice = lax.dynamic_slice_in_dim(stepped, offset, FRAG_COLS, 2)
    merged = mix_weight * stepped_slice + (1.0 - mix_weight) * new_outer_slice
    new_params = lax.dynamic_update_slice_in_dim(stepped, merged, offset, 2)
    new_outer = lax.dynamic_update_slice_in_dim(outer_params, new_outer_slice, offset, 2)
    new_outer_mom = lax.dynamic_update_slice_in_dim(outer_mom, new_mom_slice, offset, 2)
    return (new_params[None], new_moment[None], new_second[None], new_outer, new_outer_mom)


def solution(mesh):
    in_specs = (
        P("island", "fsdp", None, None),
        P("island", "fsdp", None, None),
        P("island", "fsdp", None, None),
        P("fsdp", None, None),
        P("fsdp", None, None),
        P("island", "fsdp"),
        P("island", "fsdp"),
        P(),
    )
    out_specs = (
        P("island", "fsdp", None, None),
        P("island", "fsdp", None, None),
        P("island", "fsdp", None, None),
        P("fsdp", None, None),
        P("fsdp", None, None),
    )
    return jax.shard_map(
        on_device, mesh=mesh, in_specs=in_specs, out_specs=out_specs, check_vma=False
    )
```

profile of v0, /device:TPU:0, one launch (start us, length us, event | category | flops | bytes accessed | tf_op | source)
XLA Modules:
  0.0 191.1 jit_solution(12006985125844842779)
XLA Ops:
  7.2 0.0 all-gather.2.cloned.1.call-start
  7.2 1.2 copy.61
  8.4 1.2 copy.62
  9.5 2.0 %copy.54 = bf16[1,16,2,6656]{3,1,2,0:T(8,128)(2,1)} copy(f32[1,16,2,6656]{3,2,1,0:T(2,128)} %param.8) | data formatting | bytes 1277952 | tf_op args[0]
  11.6 0.0 all-gather.2.cloned.1.call-update
  11.6 0.0 reduce-scatter.2.cloned.1.call-start
  11.6 66.3 %all-gather.2.cloned.1.call-done = bf16[128,2,6656]{2,0,1:T(8,128)(2,1)} async-done(((bf16[16,2,6656]{2,0,1:T(8,128)(2,1)}), bf16[128,2,6656]{2,0,1:T(8,128)(2,1)}) %all-gather.2.cloned.1.call-update) | async-done | bytes 3407888 | tf_op jit(solution)/shard_map/all_gather | solution.py:42
  78.0 0.0 copy-start
  78.0 3.7 %multiply_reduce_fusion.1 = (f32[512]{0:T(512)S(1)}, f32[512,6656]{1,0:T(8,128)S(1)}) fusion(bf16[128,2,6656]{2,0,1:T(8,128)(2,1)} %all-gather.2.cloned.1.call-done, s32[512]{0:T(512)} %bitcast.56), kind=kOutput, calls=%fused_computation.2 | convolution fusion | flops 879296000 | bytes 15339520 | tf_op jit(solution)/shard_map/dot_general | solution.py:43
  81.7 0.0 copy-done
  81.7 0.0 copy-start.6
  81.7 2.5 %fusion.18 = (f32[512]{0:T(512)S(1)}, f32[512,128]{0,1:T(8,128)S(1)}) fusion(bf16[128,2,6656]{2,0,1:T(8,128)(2,1)S(1)} %copy-done, f32[512,6656]{1,0:T(8,128)S(1)} %get-tuple-element.16, f32[512]{0:T(512)S(1)} %add_rsqrt_fusion), kind=kOutput, calls=%fused_computation.49 | convolution fusion | flops 879361536 | bytes 15601664 | tf_op jit(solution)/shard_map/td,ad->ta/dot_general | solution.py:49
  84.2 0.1 fusion.13
  84.3 0.0 copy-done.6
  84.3 1.5 fusion.2
  85.7 0.0 copy-start.5
  85.8 6.3 %multiply_reduce_fusion = (f32[512]{0:T(512)S(1)}, f32[512,6656]{1,0:T(8,128)}) fusion(f32[512,6656]{1,0:T(8,128)S(1)} %get-tuple-element.16, f32[512]{0:T(512)S(1)} %add_rsqrt_fusion, bf16[128,2,6656]{2,0,1:T(8,128)(2,1)S(1)} %copy-done, f32[512,128]{0,1:T(8,128)S(1)} %get-tuple-element.18, s32[512]{0:T(512)S(1)} %bitcast.59, f32[512]{0:T(512)S(1)} %fusion.13, ...), kind=kOutput, calls=%fused_computation.1 | convolution fusion | flops 886439424 | bytes 29239296 | tf_op jit(solution)/shard_map/dot_general | solution.py:55
  92.0 0.0 copy-done.5
  92.0 7.2 %fusion.1 = bf16[128,1,6656]{2,0,1:T(8,128)(2,1)S(1)} fusion(f32[512,6656]{1,0:T(8,128)} %get-tuple-element.20, f32[512,6656]{1,0:T(8,128)S(1)} %get-tuple-element.16, f32[512]{0:T(512)S(1)} %broadcast_multiply_fusion, f32[512]{0:T(512)S(1)} %add_rsqrt_fusion, s32[512]{0:T(512)S(1)} %bitcast.57), kind=kOutput, calls=%fused_computation.7 | convolution fusion | flops 893779968 | bytes 28973056 | tf_op jit(solution)/shard_map/ta,td->ad/dot_general | solution.py:62
  99.2 0.0 copy-start.1
  99.3 0.0 copy-start.4
  99.3 2.0 %pad_maximum_fusion = bf16[128,2,6656]{2,0,1:T(8,128)(2,1)} fusion(bf16[128,1,6656]{2,0,1:T(8,128)(2,1)S(1)} %fusion.2, bf16[128,1,6656]{2,0,1:T(8,128)(2,1)S(1)} %fusion.1), kind=kLoop, calls=%fused_computation.9 | loop fusion | flops 1703936 | bytes 6815744 | tf_op jit(solution)/shard_map/stack | solution.py:64
  101.3 0.0 reduce-scatter.2.cloned.1.call-update
  102.0 0.0 copy-done.1
  102.0 10.7 %psum.7 = f32[16,2,128]{2,0,1:T(8,128)S(1)} all-reduce(f32[16,2,128]{2,0,1:T(8,128)S(1)} %bitcast_subtract_fusion.1), channel_id=1, replica_groups=mesh['island'=4,'fsdp'=8] {'island'}, use_global_device_ids=true, to_apply=%region_5.0 | all-reduce | flops 4096 | bytes 32768 | tf_op jit(solution)/shard_map/psum | solution.py:34
  112.8 0.0 copy-start.3
  112.8 64.5 %reduce-scatter.2.cloned.1.call-done = bf16[16,2,6656]{2,0,1:T(8,128)(2,1)} async-done(((bf16[128,2,6656]{2,0,1:T(8,128)(2,1)}), bf16[16,2,6656]{2,0,1:T(8,128)(2,1)}) %reduce-scatter.2.cloned.1.call-update) | async-done | bytes 426000 | tf_op jit(solution)/shard_map/reduce_scatter | solution.py:63
  177.3 0.0 copy-done.4
  177.3 2.1 %fusion.12 = (f32[1,16,2,6656]{3,1,2,0:T(8,128)S(1)}, f32[16,2,6656]{2,0,1:T(8,128)S(1)}, f32[1,16,2,6656]{3,1,2,0:T(8,128)S(1)}) fusion(bf16[16,2,6656]{2,0,1:T(8,128)(2,1)} %reduce-scatter.2.cloned.1.call-done, f32[1,16,2,6656]{3,2,1,0:T(2,128)S(1)} %copy-done.4, f32[1,16,2,6656]{3,2,1,0:T(2,128)} %param.9, f32[1,16,2,6656]{3,2,1,0:T(2,128)S(1)} %copy-done.1), kind=kLoop, calls=%fused_computation.28 | loop fusion | flops 2981888 | bytes 5537792 | tf_op jit(solution)/shard_map/broadcast_in_dim | solution.py:79
  179.4 0.1 copy.55
  179.5 0.0 copy-start.2
  179.5 1.6 copy.21
  181.1 1.6 copy.22
  182.7 1.6 copy.23
  184.2 0.0 copy-done.3
  184.2 0.0 copy-done.2
  (10 shorter events, 0.1 us)
Async XLA Ops:
  7.2 70.8 %all-gather.2.cloned.1.call-start = ((), (), s32[]{:S(2)}) async-start(), calls=%async_computation.1 | async-start | bytes 3833856 | tf_op jit(solution)/shard_map/all_gather | solution.py:42
  11.6 165.7 %reduce-scatter.2.cloned.1.call-start = ((), (), s32[]{:S(2)}) async-start(), calls=%async_computation.2 | async-start | bytes 3833856 | tf_op jit(solution)/shard_map/reduce_scatter | solution.py:63
  78.0 3.7 %copy-start = (bf16[128,2,6656]{2,0,1:T(8,128)(2,1)S(1)}, bf16[128,2,6656]{2,0,1:T(8,128)(2,1)}, u32[]{:S(2)}) copy-start(bf16[128,2,6656]{2,0,1:T(8,128)(2,1)} %all-gather.2.cloned.1.call-done) | copy-start | bytes 10223620
  81.7 2.6 %copy-start.6 = (s32[1,512]{1,0:T(1,128)S(1)}, s32[1,512]{1,0:T(1,128)}, u32[]{:S(2)}) copy-start(s32[1,512]{1,0:T(1,128)} %param.14) | copy-start | bytes 6148
  85.7 6.3 %copy-start.5 = (s32[1,512]{1,0:T(1,128)S(1)}, s32[1,512]{1,0:T(1,128)}, u32[]{:S(2)}) copy-start(s32[1,512]{1,0:T(1,128)} %param.13) | copy-start | bytes 6148
  99.2 2.7 %copy-start.1 = (f32[1,16,2,6656]{3,2,1,0:T(2,128)S(1)}, f32[1,16,2,6656]{3,2,1,0:T(2,128)}, u32[]{:S(2)}) copy-start(f32[1,16,2,6656]{3,2,1,0:T(2,128)} %param.8) | copy-start | bytes 2555908
  99.3 78.1 %copy-start.4 = (f32[1,16,2,6656]{3,2,1,0:T(2,128)S(1)}, f32[1,16,2,6656]{3,2,1,0:T(2,128)}, u32[]{:S(2)}) copy-start(f32[1,16,2,6656]{3,2,1,0:T(2,128)} %param.10) | copy-start | bytes 2555908
  112.8 71.4 %copy-start.3 = (f32[16,2,6656]{2,1,0:T(2,128)}, f32[16,2,6656]{2,1,0:T(2,128)S(1)}, u32[]{:S(2)}) copy-start(f32[16,2,6656]{2,1,0:T(2,128)S(1)} %copy_dynamic-update-slice_fusion) | copy-start | bytes 2555908
  179.5 4.7 %copy-start.2 = (f32[16,2,6656]{2,1,0:T(2,128)}, f32[16,2,6656]{2,1,0:T(2,128)S(1)}, u32[]{:S(2)}) copy-start(f32[16,2,6656]{2,1,0:T(2,128)S(1)} %copy_dynamic-update-slice_fusion.1) | copy-start | bytes 2555908
Sparse Core Ops, SparseCore 0:
  11.7 66.2 all-gather.1
  101.4 75.8 reduce-scatter.1
where the time goes:
time: 191 us
  waiting for transfers between devices  131 us (69%)
  matrix products  21.1 us (11%)
  between operations  14.8 us (8%)
  blocking collectives  10.7 us (6%)
  local copies, waits for them, and re-layouts  9.22 us (5%)
  other arithmetic  4.2 us (2%)
    all_gather x1, waiting for transfers between devices, on_device(): gathered = lax.all_gather(tables_b, 'fsdp', axis=0, tiled=True)  66.3 us
    reduce_scatter x1, waiting for transfers between devices, on_device(): lax.psum_scatter(jnp.stack([embed_term, head_term], axis=1).astype(jnp.bf...  64.5 us
    psum x1, blocking collectives, on_device(): mean_drift = lax.psum(drifts, 'island') / islands  10.7 us
    unnamed x21, local copies, waits for them, and re-layouts  9.14 us
    dot_general x1, matrix products, on_device(): jnp.einsum('ta,td->ad', obs_hot, dembedded, preferred_element_type=jnp.fl...  7.21 us
    dot_general x1, matrix products, on_device(): jnp.dot(dlogits, head_rows, preferred_element_type=jnp.float32)  6.26 us
  transfers between devices with their start and end apart: 2, of which 2 were waited for; matrix products, arithmetic and copies ran while one was open for 0% of the time, Pallas kernels for 0%

commit v1 on v0

v1 whole, which is shorter than its diff:
```python
import functools
import math

import jax
import jax.numpy as jnp
from jax import lax
from jax.experimental import pallas as pl
from jax.experimental.pallas import tpu as pltpu
from jax.sharding import PartitionSpec as P

FRAG_COLS = 128
MESH = pl.DeviceIdType.MESH


beta_first = 0.8
beta_second = 0.95
inner_rate = 0.05
decay_rate = 0.1
adam_eps = 1e-08
outer_rate = 0.7
outer_beta = 0.9
mix_weight = 0.5
norm_eps = 1e-06


def dot_nt(a, b):
    return lax.dot_general(a, b, (((1,), (1,)), ((), ())), preferred_element_type=jnp.float32)


def dot_two(a, b):
    high = a.astype(jnp.bfloat16)
    low = (a - high.astype(jnp.float32)).astype(jnp.bfloat16)
    return jnp.dot(high, b, preferred_element_type=jnp.float32) + jnp.dot(
        low, b, preferred_element_type=jnp.float32
    )


def exchange_kernel(
    n, islands, blocks, width,
    tb_ref, obs_ref, act_ref, drift_ref, grad_ref, mean_ref,
    cols, count_mine, count_in, part_mine, part_in, coef_mine, coef_in,
    out_cols, grad_in, drift_in, send_sem, recv_sem, drift_send, drift_recv,
):
    me = lax.axis_index("fsdp")
    isl = lax.axis_index("island")
    rows, model_width = tb_ref.shape[1], tb_ref.shape[2]
    vocab = rows * n
    span = width * FRAG_COLS
    scale = 2.0 / math.sqrt(model_width)

    def start_of(device):
        return (blocks * device) // n

    def window(device):
        return pl.ds(pl.multiple_of(start_of(device) * FRAG_COLS, FRAG_COLS), span)

    def rows_of(device):
        return pl.ds(pl.multiple_of(device * rows, rows), rows)

    peers = [lax.rem(me + k, n) for k in range(n)]

    barrier = pltpu.get_barrier_semaphore()
    for k in range(1, n):
        pl.semaphore_signal(barrier, inc=1, device_id={"fsdp": peers[k]}, device_id_type=MESH)
    for k in range(1, islands):
        pl.semaphore_signal(
            barrier, inc=1, device_id={"island": lax.rem(isl + k, islands)}, device_id_type=MESH
        )
    pl.semaphore_wait(barrier, n - 1 + islands - 1)

    def send(phase, k, src, dst):
        copy = pltpu.make_async_remote_copy(
            src_ref=src, dst_ref=dst,
            send_sem=send_sem.at[phase, k], recv_sem=recv_sem.at[phase, k],
            device_id={"fsdp": peers[k]}, device_id_type=MESH,
        )
        copy.start()
        return copy

    order = list(range(1, n))
    first = [
        send(0, k, tb_ref.at[:, :, window(peers[k])], cols.at[:, rows_of(me), :]) for k in order
    ]
    drifts = []
    for k in range(1, islands):
        copy = pltpu.make_async_remote_copy(
            src_ref=drift_ref, dst_ref=drift_in.at[k],
            send_sem=drift_send.at[k], recv_sem=drift_recv.at[k],
            device_id={"island": lax.rem(isl + k, islands)}, device_id_type=MESH,
        )
        copy.start()
        drifts.append(copy)

    tokens = obs_ref.shape[1]
    ids = lax.broadcasted_iota(jnp.int32, (vocab, tokens), 0)
    obs_hot = (ids == obs_ref[...]).astype(jnp.float32).astype(jnp.bfloat16)
    act_hot = (ids == act_ref[...]).astype(jnp.float32).astype(jnp.bfloat16)
    count_mine[...] = dot_nt(obs_hot, act_hot)
    second = [send(1, k, count_mine.at[rows_of(peers[k])], count_in.at[k]) for k in order]

    cols[:, rows_of(me), :] = tb_ref[:, :, window(me)]
    mine = tb_ref[0].astype(jnp.float32)
    inv_rms = lax.rsqrt(
        jnp.sum(mine * mine, axis=-1, keepdims=True) * (1.0 / model_width) + norm_eps
    )

    for copy in first:
        copy.wait_recv()
    own_cols = (start_of(me + 1) - start_of(me)) * FRAG_COLS
    embed = cols[0]
    head = cols[1]
    kept = lax.broadcasted_iota(jnp.int32, (vocab, span), 1) < own_cols
    counted = jnp.where(kept, embed.astype(jnp.float32), 0.0).astype(jnp.bfloat16)
    part_mine[...] = dot_nt(counted, head)
    third = [send(2, k, part_mine.at[rows_of(peers[k])], part_in.at[k]) for k in order]

    for copy in second:
        copy.wait_recv()
    counts = count_mine[rows_of(me), :]
    for k in order:
        counts += count_in[k]
    for copy in third:
        copy.wait_recv()
    products = part_mine[rows_of(me), :]
    for k in order:
        products += part_in[k]
    logits = products * inv_rms * scale
    expon = jnp.exp(logits - jnp.max(logits, axis=-1, keepdims=True))
    probs = expon / jnp.sum(expon, axis=-1, keepdims=True)
    missed = probs.astype(jnp.bfloat16).astype(jnp.float32)
    target = (probs - 1.0).astype(jnp.bfloat16).astype(jnp.float32)
    total = jnp.sum(counts, axis=-1, keepdims=True)
    dlogits = (total - counts) * missed + counts * target
    slope = jnp.sum(dlogits * logits, axis=-1, keepdims=True) * (1.0 / model_width)
    shrink = inv_rms * inv_rms * slope
    coef_mine[0:rows, :] = dlogits * (inv_rms * scale)
    here = lax.broadcasted_iota(jnp.int32, (rows, vocab), 0) + me * rows
    lane = lax.broadcasted_iota(jnp.int32, (rows, vocab), 1)
    shrink_row = jnp.sum(jnp.where(here == lane, shrink, 0.0), axis=0, keepdims=True)
    coef_mine[rows:, :] = jnp.broadcast_to(shrink_row, (coef_mine.shape[0] - rows, vocab))
    fourth = [send(3, k, coef_mine, coef_in.at[me]) for k in order]
    coef_in[me] = coef_mine[...]

    for copy in drifts:
        copy.wait_recv()
    drift = drift_ref[...]
    for k in range(1, islands):
        drift += drift_in[k]
    mean_ref[...] = drift * (1.0 / islands)

    for copy in fourth:
        copy.wait_recv()
    coef = jnp.concatenate([coef_in[d, 0:rows, :] for d in range(n)], axis=0)
    shrinks = coef_in[0, rows : rows + 1, :]
    for d in range(1, n):
        shrinks += coef_in[d, rows : rows + 1, :]
    across = lax.broadcasted_iota(jnp.int32, (vocab, vocab), 0)
    down = lax.broadcasted_iota(jnp.int32, (vocab, vocab), 1)
    shrink_col = jnp.sum(jnp.where(across == down, shrinks, 0.0), axis=1, keepdims=True)
    embed_grad = dot_two(coef, head) - shrink_col * embed.astype(jnp.float32)
    out_cols[0] = embed_grad.astype(jnp.bfloat16)
    out_cols[1] = dot_two(coef.T, embed).astype(jnp.bfloat16)
    fifth = [send(4, k, out_cols.at[:, rows_of(peers[k]), :], grad_in.at[me]) for k in order]
    grad_in[me] = out_cols[:, rows_of(me), :]

    for copy in fifth:
        copy.wait_recv()
    for d in range(n):
        at = start_of(d) * FRAG_COLS
        size = (start_of(d + 1) - start_of(d)) * FRAG_COLS
        grad_ref[:, :, at : at + size] = grad_in[d, :, :, 0:size]
    for copy in first + second + third + fourth + fifth + drifts:
        copy.wait_send()


def exchange(tables_b, obs_ids, act_ids, drifts):
    n = lax.axis_size("fsdp")
    islands = lax.axis_size("island")
    rows, model_width = tables_b.shape[1], tables_b.shape[2]
    vocab = rows * n
    blocks = model_width // FRAG_COLS
    width = -(-blocks // n)
    span = width * FRAG_COLS
    vmem = pl.BlockSpec(memory_space=pltpu.VMEM)
    return pl.pallas_call(
        functools.partial(exchange_kernel, n, islands, blocks, width),
        out_shape=(
            jax.ShapeDtypeStruct(tables_b.shape, jnp.bfloat16),
            jax.ShapeDtypeStruct(drifts.shape, jnp.float32),
        ),
        in_specs=[vmem] * 4,
        out_specs=(vmem, vmem),
        scratch_shapes=[
            pltpu.VMEM((2, vocab, span), jnp.bfloat16),
            pltpu.VMEM((vocab, vocab), jnp.float32),
            pltpu.VMEM((n, rows, vocab), jnp.float32),
            pltpu.VMEM((vocab, vocab), jnp.float32),
            pltpu.VMEM((n, rows, vocab), jnp.float32),
            pltpu.VMEM((rows + 8, vocab), jnp.float32),
            pltpu.VMEM((n, rows + 8, vocab), jnp.float32),
            pltpu.VMEM((2, vocab, span), jnp.bfloat16),
            pltpu.VMEM((n, 2, rows, span), jnp.bfloat16),
            pltpu.VMEM((islands,) + drifts.shape, jnp.float32),
            pltpu.SemaphoreType.DMA((5, n)),
            pltpu.SemaphoreType.DMA((5, n)),
            pltpu.SemaphoreType.DMA((islands,)),
            pltpu.SemaphoreType.DMA((islands,)),
        ],
        compiler_params=pltpu.CompilerParams(
            collective_id=0, has_side_effects=True, vmem_limit_bytes=24 * 1024 * 1024
        ),
        cost_estimate=pl.CostEstimate(
            flops=10 * vocab * vocab * span, bytes_accessed=3 * tables_b.size * 2,
            transcendentals=rows * vocab,
        ),
    )(tables_b, obs_ids, act_ids, drifts)


def gathered_gradient(tables_b, obs_ids, act_ids):
    n = lax.axis_size("fsdp")
    rows, model_width = tables_b.shape[1], tables_b.shape[2]
    vocab = rows * n
    scale = 2.0 / math.sqrt(model_width)
    ids = lax.broadcasted_iota(jnp.int32, (vocab, obs_ids.shape[1]), 0)
    obs_hot = (ids == obs_ids).astype(jnp.bfloat16)
    act_hot = (ids == act_ids).astype(jnp.bfloat16)
    counts = lax.psum(dot_nt(obs_hot, act_hot), "fsdp")
    gathered = lax.all_gather(tables_b, "fsdp", axis=1, tiled=True)
    embed, head = gathered[0], gathered[1]
    wide = embed.astype(jnp.float32)
    inv_rms = lax.rsqrt(jnp.mean(wide * wide, axis=-1, keepdims=True) + norm_eps)
    logits = dot_nt(embed, head) * inv_rms * scale
    probs = jax.nn.softmax(logits, axis=-1)
    missed = probs.astype(jnp.bfloat16).astype(jnp.float32)
    target = (probs - 1.0).astype(jnp.bfloat16).astype(jnp.float32)
    total = jnp.sum(counts, axis=-1, keepdims=True)
    dlogits = (total - counts) * missed + counts * target
    slope = jnp.mean(dlogits * logits, axis=-1, keepdims=True) * (vocab / model_width)
    coef = dlogits * (inv_rms * scale)
    shrink = inv_rms * inv_rms * slope
    at = lax.axis_index("fsdp") * rows
    mine = lambda x, axis: lax.dynamic_slice_in_dim(x, at, rows, axis)
    embed_grad = dot_two(mine(coef, 0), head) - mine(shrink, 0) * mine(wide, 0)
    head_grad = dot_two(mine(coef, 1).T, embed)
    return jnp.stack([embed_grad, head_grad])


def on_device(params, adam_m, adam_v, outer_params, outer_mom, obs_ids, act_ids, fragment):
    tables = params[0]
    tables_b = jnp.swapaxes(tables.astype(jnp.bfloat16), 0, 1)
    islands = lax.axis_size("island")
    offset = fragment[0] * FRAG_COLS
    outer_slice = lax.dynamic_slice_in_dim(outer_params, offset, FRAG_COLS, 2)
    mom_slice = lax.dynamic_slice_in_dim(outer_mom, offset, FRAG_COLS, 2)
    drifts = outer_slice - lax.dynamic_slice_in_dim(tables, offset, FRAG_COLS, 2)
    if tables.shape[0] % 16 == 0:
        gradient, mean_drift = exchange(tables_b, obs_ids, act_ids, jnp.swapaxes(drifts, 0, 1))
        mean_drift = jnp.swapaxes(mean_drift, 0, 1)
    else:
        gradient = gathered_gradient(tables_b, obs_ids, act_ids)
        mean_drift = lax.psum(drifts, "island") / islands
    gradient = jnp.swapaxes(gradient, 0, 1).astype(jnp.float32)
    new_mom_slice = outer_beta * mom_slice + mean_drift
    new_outer_slice = outer_slice - outer_rate * (mean_drift + outer_beta * new_mom_slice)
    new_moment = beta_first * adam_m[0] + (1.0 - beta_first) * gradient
    new_second = beta_second * adam_v[0] + (1.0 - beta_second) * gradient * gradient
    stepped = tables - inner_rate * (
        new_moment / (jnp.sqrt(new_second) + adam_eps) + decay_rate * tables
    )
    stepped_slice = lax.dynamic_slice_in_dim(stepped, offset, FRAG_COLS, 2)
    merged = mix_weight * stepped_slice + (1.0 - mix_weight) * new_outer_slice
    new_params = lax.dynamic_update_slice_in_dim(stepped, merged, offset, 2)
    new_outer = lax.dynamic_update_slice_in_dim(outer_params, new_outer_slice, offset, 2)
    new_outer_mom = lax.dynamic_update_slice_in_dim(outer_mom, new_mom_slice, offset, 2)
    return (new_params[None], new_moment[None], new_second[None], new_outer, new_outer_mom)


def solution(mesh):
    in_specs = (
        P("island", "fsdp", None, None),
        P("island", "fsdp", None, None),
        P("island", "fsdp", None, None),
        P("fsdp", None, None),
        P("fsdp", None, None),
        P("island", "fsdp"),
        P("island", "fsdp"),
        P(),
    )
    out_specs = (
        P("island", "fsdp", None, None),
        P("island", "fsdp", None, None),
        P("island", "fsdp", None, None),
        P("fsdp", None, None),
        P("fsdp", None, None),
    )
    return jax.shard_map(
        on_device, mesh=mesh, in_specs=in_specs, out_specs=out_specs, check_vma=False
    )
```

time: 191 us -> 46.9 us (0.25)
  waiting for transfers between devices: 131 us -> 0 us
  Pallas kernels: 0 us -> 36.9 us
  matrix products: 21.1 us -> 0 us
  between operations: 14.8 us -> 1.54 us
  blocking collectives: 10.7 us -> 0 us
  other arithmetic: 4.2 us -> 0.8 us
    all_gather x1 -> x0, waiting for transfers between devices: 66.3 us -> none  [on_device(): gathered = lax.all_gather(tables_b, 'fsdp', axis=0, tiled=True)]
    reduce_scatter x1 -> x0, waiting for transfers between devices: 64.5 us -> none  [on_device(): lax.psum_scatter(jnp.stack([embed_term, head_term], axis=1).astype(jnp.bf...]
    pallas_call x0 -> x1, Pallas kernels: none -> 36.9 us  [exchange(): pl.pallas_call(functools.partial(exchange_kernel, n, islands, blocks, wid...]
    dot_general x5 -> x0, matrix products: 21.1 us -> none  [the longest x1 7.21 us: on_device(): jnp.einsum('ta,td->ad', obs_hot, dembedded, preferred_element_type=jnp.fl...]
    psum x1 -> x0, blocking collectives: 10.7 us -> none  [on_device(): mean_drift = lax.psum(drifts, 'island') / islands]
    another operation x1 -> x0, other arithmetic: 2.03 us -> none  [on_device(): jnp.stack([embed_term, head_term], axis=1).astype(jnp.bfloat16)]
    unnamed x21 -> x23, local copies, waits for them, and re-layouts: 9.14 us -> 7.41 us
  transfers between devices with their start and end apart: 2 -> 0, of which waited for: 2 -> 0; matrix products, arithmetic and copies ran while one was open for 0% -> 0% of each run, Pallas kernels for 0% -> 0%
where the time goes in v1:
time: 46.9 us; the launch traced here: 46.7 us
  Pallas kernels  36.9 us (79%)
  local copies, waits for them, and re-layouts  7.48 us (16%)
  between operations  1.54 us (3%)
  other arithmetic  0.8 us (2%)
    pallas_call x1, Pallas kernels, exchange(): pl.pallas_call(functools.partial(exchange_kernel, n, islands, blocks, wid...  36.9 us
    unnamed x23, local copies, waits for them, and re-layouts  7.41 us

profile of v1, /device:TPU:0, one launch (start us, length us, event | category | flops | bytes accessed | tf_op | source)
XLA Modules:
  0.0 46.7 jit_solution(8338345751218240663)
XLA Ops:
  0.6 0.0 copy-start.5
  0.6 1.2 %copy.63 = f32[16,2,6656]{2,1,0:T(2,128)S(1)} copy(f32[16,2,6656]{2,1,0:T(2,128)} %param.11) | data formatting | bytes 1703936
  1.9 0.2 copy-done.5
  2.0 0.0 copy-start.2
  2.0 0.0 copy-start.7
  2.0 0.1 copy.64
  2.9 0.3 copy-done.2
  3.2 0.0 copy-start.1
  3.2 0.0 copy-start.6
  3.3 0.1 copy.56
  3.4 0.0 copy-start
  3.4 0.5 %copy-done.1 = s32[1,512]{1,0:T(1,128)S(1)} copy-done((s32[1,512]{1,0:T(1,128)S(1)}, s32[1,512]{1,0:T(1,128)}, u32[]{:S(2)}) %copy-start.1) | copy-done | bytes 2072
  3.9 0.2 copy-done
  4.1 36.9 %shard_map.119 = (bf16[2,16,6656]{2,1,0:T(8,128)(2,1)S(1)}, f32[2,16,128]{2,1,0:T(8,128)S(1)}) custom-call(bf16[2,16,6656]{2,1,0:T(8,128)(2,1)S(1)} %bitcast.65, s32[1,512]{1,0:T(1,128)S(1)} %copy-done, s32[1,512]{1,0:T(1,128)S(1)} %copy-done.1, f32[2,16,128]{2,1,0:T(8,128)S(1)} %fusion.10.drift_ref), custom_call_target="tpu_custom_call" | custom-call | flops 146800640 | bytes 1277952 | tf_op jit(solution)/shard_map/pallas_call | solution.py:185
  41.0 0.0 copy-done.7
  41.0 0.0 copy-done.6
  41.0 0.8 %fusion.6 = (f32[1,16,2,6656]{3,1,2,0:T(8,128)S(1)}, f32[16,2,6656]{2,0,1:T(8,128)S(1)}, f32[1,16,2,6656]{3,1,2,0:T(8,128)S(1)}) fusion(bf16[2,16,6656]{2,1,0:T(8,128)(2,1)S(1)} %get-tuple-element.7, f32[1,16,2,6656]{3,2,1,0:T(2,128)S(1)} %copy-done.6, f32[1,16,2,6656]{3,2,1,0:T(2,128)S(1)} %copy-done.7, f32[1,16,2,6656]{3,2,1,0:T(2,128)S(1)} %copy-done.2), kind=kLoop, calls=%fused_computation.13 | loop fusion | flops 2981888 | bytes 5537792 | tf_op jit(solution)/shard_map/broadcast_in_dim | solution.py:275
  41.8 0.1 copy.57
  42.0 0.0 copy-start.3
  42.0 0.0 copy-start.4
  42.0 1.6 %copy.21 = f32[1,16,2,6656]{3,2,1,0:T(2,128)} copy(f32[1,16,2,6656]{3,1,2,0:T(8,128)S(1)} %get-tuple-element.14) | data formatting | bytes 1703936
  43.6 0.0 copy-done.3
  43.6 0.0 copy-done.4
  43.6 1.6 %copy.22 = f32[1,16,2,6656]{3,2,1,0:T(2,128)} copy(f32[1,16,2,6656]{3,1,2,0:T(8,128)S(1)} %get-tuple-element.18) | data formatting | bytes 1703936
  45.1 1.6 %copy.23 = f32[1,16,2,6656]{3,2,1,0:T(2,128)} copy(f32[1,16,2,6656]{3,1,2,0:T(8,128)S(1)} %get-tuple-element.16) | data formatting | bytes 1703936
  (7 shorter events, 0.1 us)
Async XLA Ops:
  0.6 1.4 %copy-start.5 = (f32[16,2,6656]{2,1,0:T(2,128)S(1)}, f32[16,2,6656]{2,1,0:T(2,128)}, u32[]{:S(2)}) copy-start(f32[16,2,6656]{2,1,0:T(2,128)} %param.12) | copy-start | bytes 2555908
  2.0 1.2 %copy-start.2 = (f32[1,16,2,6656]{3,2,1,0:T(2,128)S(1)}, f32[1,16,2,6656]{3,2,1,0:T(2,128)}, u32[]{:S(2)}) copy-start(f32[1,16,2,6656]{3,2,1,0:T(2,128)} %param.8) | copy-start | bytes 2555908
  2.0 39.0 %copy-start.7 = (f32[1,16,2,6656]{3,2,1,0:T(2,128)S(1)}, f32[1,16,2,6656]{3,2,1,0:T(2,128)}, u32[]{:S(2)}) copy-start(f32[1,16,2,6656]{3,2,1,0:T(2,128)} %param.9) | copy-start | bytes 2555908
  3.2 0.7 %copy-start.1 = (s32[1,512]{1,0:T(1,128)S(1)}, s32[1,512]{1,0:T(1,128)}, u32[]{:S(2)}) copy-start(s32[1,512]{1,0:T(1,128)} %act_ref.1) | copy-start | bytes 6148
  3.2 37.8 %copy-start.6 = (f32[1,16,2,6656]{3,2,1,0:T(2,128)S(1)}, f32[1,16,2,6656]{3,2,1,0:T(2,128)}, u32[]{:S(2)}) copy-start(f32[1,16,2,6656]{3,2,1,0:T(2,128)} %param.10) | copy-start | bytes 2555908
  3.4 0.8 %copy-start = (s32[1,512]{1,0:T(1,128)S(1)}, s32[1,512]{1,0:T(1,128)}, u32[]{:S(2)}) copy-start(s32[1,512]{1,0:T(1,128)} %obs_ref.1) | copy-start | bytes 6148
  42.0 1.6 %copy-start.3 = (f32[16,2,6656]{2,1,0:T(2,128)}, f32[16,2,6656]{2,1,0:T(2,128)S(1)}, u32[]{:S(2)}) copy-start(f32[16,2,6656]{2,1,0:T(2,128)S(1)} %get-tuple-element.20) | copy-start | bytes 2555908
  42.0 1.6 %copy-start.4 = (f32[16,2,6656]{2,1,0:T(2,128)}, f32[16,2,6656]{2,1,0:T(2,128)S(1)}, u32[]{:S(2)}) copy-start(f32[16,2,6656]{2,1,0:T(2,128)S(1)} %get-tuple-element.19) | copy-start | bytes 2555908
